TPU v7x, 32 devices: a whole 2x2x4 slice. The times are simulated.
32 devices in a mesh: parts: 2 (over x), wide: 8 (over z, y), loop: 2 (over core).
Axes of the slice: x: 2, y: 2, z: 4, core: 2. Of those that a mesh axis runs over, the one named last changes fastest.
Arguments:
- density: bfloat16 [37, 32768], P(None, ('parts', 'wide', 'loop')), parts along dimension 1, may hold values from -6 to 6
- near_blocks: bfloat16 [128, 8, 256, 256], P(('parts', 'wide', 'loop')), parts along dimension 0, may hold values from -0.125 to 0.125
- near_source: int32 [128, 8], P(('parts', 'wide', 'loop')), parts along dimension 0, may hold values from 0 to 7
- source_basis: bfloat16 [128, 64, 256], P(('parts', 'wide', 'loop')), parts along dimension 0, may hold values from -0.375 to 0.375
- cluster_of: int32 [128], P(('parts', 'wide', 'loop')), parts along dimension 0, may hold values from 0 to 1
- translation: bfloat16 [4096, 2048], P(('parts', 'wide', 'loop')), parts along dimension 0, may hold values from -0.125 to 0.125
- eval_basis: bfloat16 [128, 64, 256], P(('parts', 'wide', 'loop')), parts along dimension 0, may hold values from -0.75 to 0.75
Outputs:
- powers: bfloat16 [4, 37, 32768], P(None, None, ('parts', 'wide', 'loop')), parts along dimension 2
There are 2 independent parts, one for each index of `parts`. A program takes and returns all parts, laid end to end along the dimension named above; each array names one. Nothing has to cross between parts.
All inputs are finite; a program needn't handle non-finite values.
Results may differ from a plain program's by a relative error of at most 0.011.
Values may be sent and summed in bfloat16 or wider, within the bound.
A program may use at most 64 MiB of HBM per device.

v0:
```python
import jax
import jax.numpy as jnp
from jax import lax
from jax.sharding import PartitionSpec as P

R = 64
CL_DEV = 2
APPLIES = 4


def shifted(value, axis, steps):
    count = lax.axis_size(axis)
    pairs = [(source, (source + steps) % count) for source in range(count)]
    return lax.ppermute(value, axis, pairs)


def per_device(
    density, near_blocks, near_source, source_basis, cluster_of, translation, eval_basis
):
    rows = density.shape[0]
    count = near_blocks.shape[0]
    elements = near_blocks.shape[2]
    member = (cluster_of[:, None] == jnp.arange(CL_DEV, dtype=jnp.int32)[None, :]).astype(
        jnp.float32
    )
    member_low = member.astype(jnp.bfloat16)
    current = density
    results = []
    for number in range(APPLIES):
        own = current.reshape(rows, count, elements)
        loops = lax.axis_size("loop")
        here = lax.axis_index("loop")
        pieces = [own]
        pieces.append(shifted(own, "loop", 1))
        group = jnp.concatenate(pieces, axis=1)
        owner = near_source // count
        rotated = (here - owner) % loops * count + near_source % count
        selected = group[:, rotated, :]
        near = jnp.einsum(
            "kpnb,pnab->kpa", selected, near_blocks, preferred_element_type=jnp.float32
        )
        coefficients = jnp.einsum(
            "kpb,prb->kpr", own, source_basis, preferred_element_type=jnp.float32
        )
        local_coeffs = jnp.sum(coefficients[:, :, None, :] * member[None, :, :, None], axis=1)
        local_coeffs = local_coeffs.astype(jnp.bfloat16).reshape(rows, CL_DEV * R)
        total = lax.dot_general(
            lax.all_gather(local_coeffs, ("wide", "loop"), axis=1, tiled=True),
            translation,
            (((1,), (1,)), ((), ())),
            preferred_element_type=jnp.float32,
        )
        expansion = total.astype(jnp.bfloat16).reshape(rows, CL_DEV, R)
        picked = jnp.einsum(
            "kcr,pc->kpr", expansion, member_low, preferred_element_type=jnp.float32
        ).astype(jnp.bfloat16)
        far = jnp.einsum("kpr,pra->kpa", picked, eval_basis, preferred_element_type=jnp.float32)
        current = (near + far).astype(jnp.bfloat16).reshape(rows, count * elements)
        results.append(current)
    return jnp.stack(results, axis=0)


def solution(mesh):
    return jax.shard_map(
        per_device,
        mesh=mesh,
        in_specs=(
            P(None, ("parts", "wide", "loop")),
            P(("parts", "wide", "loop"), None, None, None),
            P(("parts", "wide", "loop"), None),
            P(("parts", "wide", "loop"), None, None),
            P(("parts", "wide", "loop")),
            P(("parts", "wide", "loop"), None),
            P(("parts", "wide", "loop"), None, None),
        ),
        out_specs=P(None, None, ("parts", "wide", "loop")),
        check_vma=False,
    )
```

profile of v0, /device:TPU:0, one launch (start us, length us, event | category | flops | bytes accessed | tf_op | source)
XLA Modules:
  0.0 107.6 jit_solution(10197078989949315592)
XLA Ops:
  0.0 1.0 reshape.52
  1.0 0.5 collective-permute-start
  1.5 0.7 compare_select_fusion
  2.3 0.7 compare_convert_fusion
  3.0 1.1 convolution_bitcast_fusion.7
  4.1 0.2 multiply_reduce_fusion.3
  4.3 0.1 convert_element_type.101
  4.4 23.1 %all_gather.12 = bf16[37,2048]{1,0:T(8,128)(2,1)S(1)} all-gather(bf16[37,128]{1,0:T(8,128)(2,1)S(1)} %convert_element_type.101), channel_id=1, replica_groups=mesh['parts'=2,'wide'=8,'loop'=2] {'wide','loop'}, dimensions={1}, use_global_device_ids=true | all-gather | bytes 161024 | tf_op jit(solution)/shard_map/all_gather | solution.py:48
  27.4 0.3 convolution_convert_fusion.7
  27.7 0.1 reshape.53
  27.8 0.9 fusion.12
  28.7 1.0 fusion.22
  29.8 0.6 gather_fusion
  30.5 3.6 %fusion.11 = bf16[37,4,256]{2,0,1:T(8,128)(2,1)S(1)} fusion(f32[4,37,256]{2,1,0:T(8,128)S(1)} %fusion.22, bf16[37,4,8,256]{3,0,2,1:T(8,128)(2,1)S(1)} %bitcast.113, bf16[4,8,256,256]{3,2,1,0:T(8,128)(2,1)} %param.8), kind=kOutput, calls=%fused_computation.19 | convolution fusion | flops 155265024 | bytes 5027840 | tf_op jit(solution)/shard_map/kpnb,pnab->kpa/dot_general | solution.py:39
  34.0 0.4 collective-permute-start.1
  34.4 0.1 convolution_bitcast_fusion.6
  34.6 0.2 multiply_reduce_fusion.2
  34.8 0.1 convert_element_type.108
  34.9 17.7 %all_gather.13 = bf16[37,2048]{1,0:T(8,128)(2,1)S(1)} all-gather(bf16[37,128]{1,0:T(8,128)(2,1)S(1)} %convert_element_type.108), channel_id=1, replica_groups=mesh['parts'=2,'wide'=8,'loop'=2] {'wide','loop'}, dimensions={1}, use_global_device_ids=true | all-gather | bytes 161024 | tf_op jit(solution)/shard_map/all_gather | solution.py:48
  52.6 0.3 convolution_convert_fusion.6
  52.9 0.1 reshape.54
  53.0 0.2 fusion.13
  53.2 0.1 fusion.20
  53.5 0.6 gather_fusion.1
  54.1 3.5 %fusion.10 = bf16[37,4,256]{2,0,1:T(8,128)(2,1)S(1)} fusion(f32[4,37,256]{2,1,0:T(8,128)S(1)} %fusion.20, bf16[37,4,8,256]{3,0,2,1:T(8,128)(2,1)S(1)} %bitcast.114, bf16[4,8,256,256]{3,2,1,0:T(8,128)(2,1)} %param.8), kind=kOutput, calls=%fused_computation.18 | convolution fusion | flops 155265024 | bytes 5027840 | tf_op jit(solution)/shard_map/kpnb,pnab->kpa/dot_general | solution.py:39
  57.6 0.4 collective-permute-start.2
  58.0 0.1 convolution_bitcast_fusion.5
  58.2 0.2 multiply_reduce_fusion.1
  58.4 0.1 convert_element_type.115
  58.5 19.4 %all_gather.14 = bf16[37,2048]{1,0:T(8,128)(2,1)S(1)} all-gather(bf16[37,128]{1,0:T(8,128)(2,1)S(1)} %convert_element_type.115), channel_id=1, replica_groups=mesh['parts'=2,'wide'=8,'loop'=2] {'wide','loop'}, dimensions={1}, use_global_device_ids=true | all-gather | bytes 161024 | tf_op jit(solution)/shard_map/all_gather | solution.py:48
  77.9 0.3 convolution_convert_fusion.5
  78.2 0.1 reshape.55
  78.3 0.2 fusion.14
  78.5 0.2 fusion.18
  78.8 0.6 gather_fusion.2
  79.4 3.5 %fusion.9 = bf16[37,4,256]{2,0,1:T(8,128)(2,1)S(1)} fusion(f32[4,37,256]{2,1,0:T(8,128)S(1)} %fusion.18, bf16[37,4,8,256]{3,0,2,1:T(8,128)(2,1)S(1)} %bitcast.115, bf16[4,8,256,256]{3,2,1,0:T(8,128)(2,1)} %param.8), kind=kOutput, calls=%fused_computation.17 | convolution fusion | flops 155265024 | bytes 5027840 | tf_op jit(solution)/shard_map/kpnb,pnab->kpa/dot_general | solution.py:39
  82.9 0.4 collective-permute-start.3
  83.3 0.1 convolution_bitcast_fusion.4
  83.5 0.2 multiply_reduce_fusion
  83.7 0.1 convert_element_type.122
  83.8 17.7 %all_gather.15 = bf16[37,2048]{1,0:T(8,128)(2,1)S(1)} all-gather(bf16[37,128]{1,0:T(8,128)(2,1)S(1)} %convert_element_type.122), channel_id=1, replica_groups=mesh['parts'=2,'wide'=8,'loop'=2] {'wide','loop'}, dimensions={1}, use_global_device_ids=true | all-gather | bytes 161024 | tf_op jit(solution)/shard_map/all_gather | solution.py:48
  101.5 0.3 convolution_convert_fusion.4
  101.8 0.1 reshape.56
  101.9 0.2 fusion.15
  102.1 0.1 fusion.16
  102.4 0.6 gather_fusion.3
  103.0 3.5 %fusion.8 = bf16[37,4,256]{2,0,1:T(8,128)(2,1)S(1)} fusion(f32[4,37,256]{2,1,0:T(8,128)S(1)} %fusion.16, bf16[37,4,8,256]{3,0,2,1:T(8,128)(2,1)S(1)} %bitcast.112, bf16[4,8,256,256]{3,2,1,0:T(8,128)(2,1)} %param.8), kind=kOutput, calls=%fused_computation.16 | convolution fusion | flops 155265024 | bytes 5027840 | tf_op jit(solution)/shard_map/kpnb,pnab->kpa/dot_general | solution.py:39
  106.6 1.0 copy.55
  (32 shorter events, 0.7 us)
Async XLA Ops:
  0.0 27.4 %copy-start = (bf16[128,2048]{1,0:T(8,128)(2,1)S(1)}, bf16[128,2048]{1,0:T(8,128)(2,1)}, u32[]{:S(2)}) copy-start(bf16[128,2048]{1,0:T(8,128)(2,1)} %param.12) | copy-start | bytes 1572868
  1.0 28.8 %collective-permute-start = (bf16[37,4,256]{2,0,1:T(8,128)(2,1)S(1)}, bf16[37,4,256]{2,0,1:T(8,128)(2,1)S(1)}, u32[]{:S(2)}, u32[]{:S(2)}) collective-permute-start(bf16[37,4,256]{2,0,1:T(8,128)(2,1)S(1)} %copy.41), channel_id=1, source_target_pairs={{0,1},{1,0},{2,3},{3,2},{4,5},{5,4},{6,7},{7,6},{8,9},{9,8},{10,11... | collective-permute-start | bytes 227336 | tf_op jit(solution)/shard_map/ppermute | solution.py:14
  29.8 4.6 %copy-start.1 = (bf16[4,64,256]{2,1,0:T(8,128)(2,1)S(1)}, bf16[4,64,256]{2,1,0:T(8,128)(2,1)}, u32[]{:S(2)}) copy-start(bf16[4,64,256]{2,1,0:T(8,128)(2,1)} %param.10) | copy-start | bytes 393220
  30.4 22.6 %copy-start.3 = (s32[4]{0:T(128)S(1)}, s32[4]{0:T(128)}, u32[]{:S(2)}) copy-start(s32[4]{0:T(128)} %param.11) | copy-start | bytes 52
  30.4 22.8 %copy-start.2 = (bf16[4,64,256]{2,1,0:T(8,128)(2,1)S(1)}, bf16[4,64,256]{2,1,0:T(8,128)(2,1)}, u32[]{:S(2)}) copy-start(bf16[4,64,256]{2,1,0:T(8,128)(2,1)} %param.13) | copy-start | bytes 393220
  34.0 19.4 %collective-permute-start.1 = (bf16[37,4,256]{2,0,1:T(8,128)(2,1)S(1)}, bf16[37,4,256]{2,0,1:T(8,128)(2,1)S(1)}, u32[]{:S(2)}, u32[]{:S(2)}) collective-permute-start(bf16[37,4,256]{2,0,1:T(8,128)(2,1)S(1)} %fusion.11), channel_id=1, source_target_pairs={{0,1},{1,0},{2,3},{3,2},{4,5},{5,4},{6,7},{7,6},{8,9},{9,8},{10,11... | collective-permute-start | bytes 227336 | tf_op jit(solution)/shard_map/ppermute | solution.py:14
  57.6 21.1 %collective-permute-start.2 = (bf16[37,4,256]{2,0,1:T(8,128)(2,1)S(1)}, bf16[37,4,256]{2,0,1:T(8,128)(2,1)S(1)}, u32[]{:S(2)}, u32[]{:S(2)}) collective-permute-start(bf16[37,4,256]{2,0,1:T(8,128)(2,1)S(1)} %fusion.10), channel_id=1, source_target_pairs={{0,1},{1,0},{2,3},{3,2},{4,5},{5,4},{6,7},{7,6},{8,9},{9,8},{10,11... | collective-permute-start | bytes 227336 | tf_op jit(solution)/shard_map/ppermute | solution.py:14
  82.9 19.4 %collective-permute-start.3 = (bf16[37,4,256]{2,0,1:T(8,128)(2,1)S(1)}, bf16[37,4,256]{2,0,1:T(8,128)(2,1)S(1)}, u32[]{:S(2)}, u32[]{:S(2)}) collective-permute-start(bf16[37,4,256]{2,0,1:T(8,128)(2,1)S(1)} %fusion.9), channel_id=1, source_target_pairs={{0,1},{1,0},{2,3},{3,2},{4,5},{5,4},{6,7},{7,6},{8,9},{9,8},{10,11... | collective-permute-start | bytes 227336 | tf_op jit(solution)/shard_map/ppermute | solution.py:14
where the time goes:
time: 108 us
  blocking collectives  77.8 us (72%)
  matrix products  19.8 us (18%)
  local copies, waits for them, and re-layouts  5.63 us (5%)
  other arithmetic  2.26 us (2%)
  starting transfers between devices  1.75 us (2%)
    all_gather x4, blocking collectives, per_device(): lax.all_gather(local_coeffs, ('wide', 'loop'), axis=1, tiled=True)  77.8 us
    dot_general x4, matrix products, per_device(): jnp.einsum('kpnb,pnab->kpa', selected, near_blocks, preferred_element_typ...  14.1 us
    gather x4, local copies, waits for them, and re-layouts, per_device(): selected = group[:, rotated, :]  2.37 us
  transfers between devices with their start and end apart: 4, of which 0 were waited for; matrix products, arithmetic and copies ran while one was open for 8% of the time, Pallas kernels for 0%

commit v1 on v0

v1 whole, which is shorter than its diff:
```python
import functools

import jax
import jax.numpy as jnp
from jax import lax
from jax.experimental import pallas as pl
from jax.experimental.pallas import tpu as pltpu
from jax.sharding import PartitionSpec as P

CL_DEV = 2
APPLIES = 4
MESH = pl.DeviceIdType.MESH
NT = (((1,), (1,)), ((), ()))


def dot_nt(a, b):
    return lax.dot_general(a, b, NT, preferred_element_type=jnp.float32)


def kernel(
    wides, loops, count,
    clusters, sources, density, near_hbm, source_hbm, translation_hbm, eval_hbm,
    out,
    field0, field1, field2, field3, gathered, near_vmem, source_vmem, translation_vmem,
    eval_vmem, source_all, eval_all, near_sum,
    load_sem, field_send, field_recv, block_send, block_recv, pass_send, pass_recv,
):
    fields = (field0, field1, field2, field3)
    wide = lax.axis_index("wide")
    loop = lax.axis_index("loop")
    other = 1 - loop
    rows = density.shape[0]
    padded, elements = field0.shape[1:]
    near_count = sources.shape[1]
    rank = source_hbm.shape[1]
    width = CL_DEV * rank

    def peer(step):
        return lax.rem(wide + step, wides)

    loads = [
        pltpu.make_async_copy(source_hbm, source_vmem, load_sem.at[0]),
        pltpu.make_async_copy(eval_hbm, eval_vmem, load_sem.at[1]),
        pltpu.make_async_copy(near_hbm, near_vmem, load_sem.at[2]),
        pltpu.make_async_copy(translation_hbm, translation_vmem, load_sem.at[3]),
    ]
    for load in loads:
        load.start()

    barrier = pltpu.get_barrier_semaphore()
    pl.semaphore_signal(barrier, inc=1, device_id={"loop": other}, device_id_type=MESH)

    def greet(step, carry):
        pl.semaphore_signal(
            barrier, inc=1, device_id={"wide": peer(step)}, device_id_type=MESH
        )
        return carry

    lax.fori_loop(1, wides, greet, 0)

    mine = loop * count
    for p in range(count):
        field0[mine + p] = jnp.zeros((padded, elements), jnp.bfloat16)
        field0[mine + p, 0:rows, :] = density[:, p * elements : (p + 1) * elements]
    loads[0].wait()
    loads[1].wait()
    for p in range(count):
        for c in range(CL_DEV):
            chosen = clusters[0, p] == c
            source_all[c * rank : (c + 1) * rank, p * elements : (p + 1) * elements] = jnp.where(
                chosen, source_vmem[p], jnp.zeros((rank, elements), jnp.bfloat16)
            )
            eval_all[c * rank : (c + 1) * rank, p * elements : (p + 1) * elements] = jnp.where(
                chosen, eval_vmem[p], jnp.zeros((rank, elements), jnp.bfloat16)
            )
    pl.semaphore_wait(barrier, wides)

    def field_copy(j):
        part = fields[j].at[pl.ds(mine, count)]
        return pltpu.make_async_remote_copy(
            src_ref=part, dst_ref=part, send_sem=field_send.at[j], recv_sem=field_recv.at[j],
            device_id={"loop": other}, device_id_type=MESH,
        )

    def block_copy(j, step):
        block = gathered.at[j, loop, wide]
        return pltpu.make_async_remote_copy(
            src_ref=block, dst_ref=block, send_sem=block_send.at[j], recv_sem=block_recv.at[j, step],
            device_id={"wide": peer(step)}, device_id_type=MESH,
        )

    def arrived(j, step):
        block = gathered.at[j, loop, lax.rem(wide - step + wides, wides)]
        return pltpu.make_async_remote_copy(
            src_ref=block, dst_ref=block, send_sem=block_send.at[j], recv_sem=block_recv.at[j, step],
            device_id={"wide": peer(step)}, device_id_type=MESH,
        )

    def pass_copy(j, step):
        block = gathered.at[j, loop, lax.rem(wide - step + wides, wides)]
        return pltpu.make_async_remote_copy(
            src_ref=block, dst_ref=block, send_sem=pass_send.at[j], recv_sem=pass_recv.at[j],
            device_id={"loop": other}, device_id_type=MESH,
        )

    def each(first, last, body):
        if wides <= 8:
            for step in range(first, last):
                body(step)
        else:
            lax.fori_loop(first, last, lambda step, carry: (body(step), carry)[1], 0)

    for j in range(APPLIES):
        field = fields[j]
        field_copy(j).start()
        own = jnp.concatenate([field[mine + p] for p in range(count)], axis=1)
        gathered[j, loop, wide] = dot_nt(own, source_all[...]).astype(jnp.bfloat16)

        def send(step):
            block_copy(j, step).start()

        each(1, wides, send)
        pass_copy(j, 0).start()

        field_copy(j).wait_recv()
        if j == 0:
            loads[2].wait()
        for p in range(count):
            total = None
            for n in range(near_count):
                term = dot_nt(field[sources[p, n]], near_vmem[p, n])
                total = term if total is None else total + term
            near_sum[p] = total

        def forward(step):
            arrived(j, step).wait_recv()
            pass_copy(j, step).start()

        each(1, wides, forward)
        if j == 0:
            loads[3].wait()
        whole = gathered.at[j, other]
        pltpu.make_async_remote_copy(
            src_ref=whole, dst_ref=whole, send_sem=pass_send.at[j], recv_sem=pass_recv.at[j],
            device_id={"loop": other}, device_id_type=MESH,
        ).wait_recv()
        total = None
        chunk = 8
        for start in range(0, wides, chunk):
            here = range(start, min(start + chunk, wides))
            blocks = [gathered[j, l, w] for w in here for l in range(loops)]
            columns = slice(start * loops * width, (here[-1] + 1) * loops * width)
            term = dot_nt(jnp.concatenate(blocks, axis=1), translation_vmem[:, columns])
            total = term if total is None else total + term
        expansion = total.astype(jnp.bfloat16)
        for p in range(count):
            far = jnp.dot(
                expansion, eval_all[:, p * elements : (p + 1) * elements],
                preferred_element_type=jnp.float32,
            )
            value = (near_sum[p] + far).astype(jnp.bfloat16)
            if j + 1 < APPLIES:
                fields[j + 1][mine + p] = value
            out[j, :, p * elements : (p + 1) * elements] = value[:rows]

    for j in range(APPLIES):
        field_copy(j).wait_send()
        every = gathered.at[j, loop]
        most = gathered.at[j, loop, pl.ds(0, wides - 1)]
        for ref, sem in ((every, pass_send), (most, block_send)):
            pltpu.make_async_remote_copy(
                src_ref=ref, dst_ref=ref, send_sem=sem.at[j], recv_sem=pass_recv.at[j],
                device_id={"loop": other}, device_id_type=MESH,
            ).wait_send()


def per_device(
    density, near_blocks, near_source, source_basis, cluster_of, translation, eval_basis
):
    wides, loops = lax.axis_size("wide"), lax.axis_size("loop")
    rows, size = density.shape
    count, near_count, elements, _ = near_blocks.shape
    rank = source_basis.shape[1]
    width = CL_DEV * rank
    padded = -(-rows // 16) * 16
    vmem = pl.BlockSpec(memory_space=pltpu.VMEM)
    smem = pl.BlockSpec(memory_space=pltpu.SMEM)
    anywhere = pl.BlockSpec(memory_space=pl.ANY)
    low, full = jnp.bfloat16, jnp.float32
    return pl.pallas_call(
        functools.partial(kernel, wides, loops, count),
        out_shape=jax.ShapeDtypeStruct((APPLIES, rows, size), low),
        in_specs=[smem, smem, vmem, anywhere, anywhere, anywhere, anywhere],
        out_specs=vmem,
        scratch_shapes=[pltpu.VMEM((loops * count, padded, elements), low)] * APPLIES
        + [
            pltpu.VMEM((APPLIES, loops, wides, padded, width), low),
            pltpu.VMEM(near_blocks.shape, low),
            pltpu.VMEM(source_basis.shape, low),
            pltpu.VMEM(translation.shape, low),
            pltpu.VMEM(eval_basis.shape, low),
            pltpu.VMEM((width, size), low),
            pltpu.VMEM((width, size), low),
            pltpu.VMEM((count, padded, elements), full),
            pltpu.SemaphoreType.DMA((4,)),
            pltpu.SemaphoreType.DMA((APPLIES,)),
            pltpu.SemaphoreType.DMA((APPLIES,)),
            pltpu.SemaphoreType.DMA((APPLIES,)),
            pltpu.SemaphoreType.DMA((APPLIES, wides)),
            pltpu.SemaphoreType.DMA((APPLIES,)),
            pltpu.SemaphoreType.DMA((APPLIES,)),
        ],
        compiler_params=pltpu.CompilerParams(
            collective_id=0, has_side_effects=True, vmem_limit_bytes=40 * 2**20
        ),
        name="apply_operator",
    )(
        cluster_of.reshape(1, count), near_source, density, near_blocks, source_basis,
        translation, eval_basis,
    )


def solution(mesh):
    split = ("parts", "wide", "loop")
    return jax.shard_map(
        per_device,
        mesh=mesh,
        in_specs=(
            P(None, split),
            P(split, None, None, None),
            P(split, None),
            P(split, None, None),
            P(split),
            P(split, None),
            P(split, None, None),
        ),
        out_specs=P(None, None, split),
        check_vma=False,
    )
```

time: 108 us -> 39.5 us (0.37)
  blocking collectives: 77.8 us -> 0 us
  Pallas kernels: 0 us -> 31 us
  matrix products: 19.8 us -> 0 us
  local copies, waits for them, and re-layouts: 5.63 us -> 8.21 us
  other arithmetic: 2.26 us -> 0 us
  starting transfers between devices: 1.75 us -> 0 us
    all_gather x4 -> x0, blocking collectives: 77.8 us -> none  [per_device(): lax.all_gather(local_coeffs, ('wide', 'loop'), axis=1, tiled=True)]
    pallas_call x0 -> x1, Pallas kernels: none -> 31 us  [per_device(): pl.pallas_call(functools.partial(kernel, wides, loops, count), out_shape=...]
    dot_general x20 -> x0, matrix products: 19.8 us -> none  [the longest x4 14.1 us: per_device(): jnp.einsum('kpnb,pnab->kpa', selected, near_blocks, preferred_element_typ...]
    unnamed x8 -> x14, local copies, waits for them, and re-layouts: 0.02 us -> 7.26 us
    gather x4 -> x0, local copies, waits for them, and re-layouts: 2.37 us -> none  [per_device(): selected = group[:, rotated, :]]
    ppermute x4 -> x0, starting transfers between devices: 1.75 us -> none  [shifted(): return lax.ppermute(value, axis, pairs)]
    reshape x6 -> x0, local copies, waits for them, and re-layouts: 1.37 us -> none  [the longest x2 0.99 us: per_device(): own = current.reshape(rows, count, elements)]
    another operation x5 -> x0, local copies, waits for them, and re-layouts: 1.11 us -> none  [per_device(): return jnp.stack(results, axis=0)]
  transfers between devices with their start and end apart: 4 -> 0, of which waited for: 0 -> 0; matrix products, arithmetic and copies ran while one was open for 8% -> 0% of each run, Pallas kernels for 0% -> 0%
where the time goes in v1:
time: 39.5 us; the launch traced here: 39.2 us
  Pallas kernels  31 us (78%)
  local copies, waits for them, and re-layouts  8.21 us (21%)
    pallas_call x1, Pallas kernels, per_device(): pl.pallas_call(functools.partial(kernel, wides, loops, count), out_shape=...  31 us
    unnamed x14, local copies, waits for them, and re-layouts  7.26 us
    pallas_call x1, local copies, waits for them, and re-layouts, per_device(): pl.pallas_call(functools.partial(kernel, wides, loops, count), out_shape=...  0.96 us

profile of v1, /device:TPU:0, one launch (start us, length us, event | category | flops | bytes accessed | tf_op | source)
XLA Modules:
  0.0 39.2 jit_solution(10675417227393113334)
XLA Ops:
  0.0 0.0 copy-start
  0.0 2.2 %copy-done = bf16[4,8,256,256]{3,2,1,0:T(8,128)(2,1)S(1)} copy-done((bf16[4,8,256,256]{3,2,1,0:T(8,128)(2,1)S(1)}, bf16[4,8,256,256]{3,2,1,0:T(8,128)(2,1)}, u32[]{:S(2)}) %copy-start) | copy-done | bytes 4194328
  2.2 0.0 copy-start.1
  2.2 1.0 %copy-done.1 = bf16[128,2048]{1,0:T(8,128)(2,1)S(1)} copy-done((bf16[128,2048]{1,0:T(8,128)(2,1)S(1)}, bf16[128,2048]{1,0:T(8,128)(2,1)}, u32[]{:S(2)}) %copy-start.1) | copy-done | bytes 524312
  3.2 0.0 copy-start.2
  3.2 0.9 %copy-done.2 = bf16[4,64,256]{2,1,0:T(8,128)(2,1)S(1)} copy-done((bf16[4,64,256]{2,1,0:T(8,128)(2,1)S(1)}, bf16[4,64,256]{2,1,0:T(8,128)(2,1)}, u32[]{:S(2)}) %copy-start.2) | copy-done | bytes 131096
  4.1 0.0 copy-start.3
  4.1 0.9 %copy-done.3 = bf16[4,64,256]{2,1,0:T(8,128)(2,1)S(1)} copy-done((bf16[4,64,256]{2,1,0:T(8,128)(2,1)S(1)}, bf16[4,64,256]{2,1,0:T(8,128)(2,1)}, u32[]{:S(2)}) %copy-start.3) | copy-done | bytes 131096
  5.0 0.0 copy-start.4
  5.0 0.9 %copy-done.4 = bf16[37,1024]{1,0:T(8,128)(2,1)S(1)} copy-done((bf16[37,1024]{1,0:T(8,128)(2,1)S(1)}, bf16[37,1024]{1,0:T(8,128)(2,1)}, u32[]{:S(2)}) %copy-start.4) | copy-done | bytes 75800
  5.9 0.0 copy-start.5
  5.9 0.7 %copy-done.5 = s32[4,8]{1,0:T(4,128)S(1)} copy-done((s32[4,8]{1,0:T(4,128)S(1)}, s32[4,8]{1,0:T(4,128)}, u32[]{:S(2)}) %copy-start.5) | copy-done | bytes 152
  6.6 0.0 copy-start.6
  6.6 0.7 %copy-done.6 = s32[4]{0:T(128)S(1)} copy-done((s32[4]{0:T(128)S(1)}, s32[4]{0:T(128)}, u32[]{:S(2)}) %copy-start.6) | copy-done | bytes 40
  7.3 31.0 %apply_operator.1 = bf16[4,37,1024]{2,1,0:T(8,128)(2,1)S(1)} custom-call(s32[1,4]{1,0:T(1,128)S(1)} %bitcast.1, s32[4,8]{1,0:T(4,128)S(1)} %copy-done.5, bf16[37,1024]{1,0:T(8,128)(2,1)S(1)} %copy-done.4, bf16[4,8,256,256]{3,2,1,0:T(8,128)(2,1)S(1)} %copy-done, bf16[4,64,256]{2,1,0:T(8,128)(2,1)S(1)} %copy-done.2, bf16[128,2048]{1,0:T(8,128)(2,1)S(1)} %copy-done.1, ...), custom_call_target="tpu_custom_call" | custom-call | tf_op jit(solution)/shard_map/apply_operator/pallas_call | solution.py:190
  38.3 1.0 %copy.8 = bf16[4,37,1024]{2,0,1:T(4,128)(2,1)} copy(bf16[4,37,1024]{2,1,0:T(8,128)(2,1)S(1)} %apply_operator.1) | data formatting | bytes 606208 | tf_op jit(solution)/shard_map/apply_operator/pallas_call | solution.py:190
Async XLA Ops:
  0.0 2.2 %copy-start = (bf16[4,8,256,256]{3,2,1,0:T(8,128)(2,1)S(1)}, bf16[4,8,256,256]{3,2,1,0:T(8,128)(2,1)}, u32[]{:S(2)}) copy-start(bf16[4,8,256,256]{3,2,1,0:T(8,128)(2,1)} %near_hbm.1) | copy-start | bytes 12582916
  2.2 1.0 %copy-start.1 = (bf16[128,2048]{1,0:T(8,128)(2,1)S(1)}, bf16[128,2048]{1,0:T(8,128)(2,1)}, u32[]{:S(2)}) copy-start(bf16[128,2048]{1,0:T(8,128)(2,1)} %translation_hbm.1) | copy-start | bytes 1572868
  3.2 0.9 %copy-start.2 = (bf16[4,64,256]{2,1,0:T(8,128)(2,1)S(1)}, bf16[4,64,256]{2,1,0:T(8,128)(2,1)}, u32[]{:S(2)}) copy-start(bf16[4,64,256]{2,1,0:T(8,128)(2,1)} %source_hbm.1) | copy-start | bytes 393220
  4.1 0.9 %copy-start.3 = (bf16[4,64,256]{2,1,0:T(8,128)(2,1)S(1)}, bf16[4,64,256]{2,1,0:T(8,128)(2,1)}, u32[]{:S(2)}) copy-start(bf16[4,64,256]{2,1,0:T(8,128)(2,1)} %eval_hbm.1) | copy-start | bytes 393220
  5.0 0.9 %copy-start.4 = (bf16[37,1024]{1,0:T(8,128)(2,1)S(1)}, bf16[37,1024]{1,0:T(8,128)(2,1)}, u32[]{:S(2)}) copy-start(bf16[37,1024]{1,0:T(8,128)(2,1)} %density.1) | copy-start | bytes 227332
  5.9 0.7 %copy-start.5 = (s32[4,8]{1,0:T(4,128)S(1)}, s32[4,8]{1,0:T(4,128)}, u32[]{:S(2)}) copy-start(s32[4,8]{1,0:T(4,128)} %sources.1) | copy-start | bytes 388
  6.6 0.7 %copy-start.6 = (s32[4]{0:T(128)S(1)}, s32[4]{0:T(128)}, u32[]{:S(2)}) copy-start(s32[4]{0:T(128)} %param.11) | copy-start | bytes 52

commit v2 on v1

--- a/solution.py
+++ b/solution.py
@@ -19,10 +19,10 @@
 
 def kernel(
     wides, loops, count,
-    clusters, sources, density, near_hbm, source_hbm, translation_hbm, eval_hbm,
+    clusters_hbm, sources_hbm, density_hbm, near_hbm, source_hbm, translation_hbm, eval_hbm,
     out,
     field0, field1, field2, field3, gathered, near_vmem, source_vmem, translation_vmem,
-    eval_vmem, source_all, eval_all, near_sum,
+    eval_vmem, density, clusters, sources, source_all, eval_all, near_sum,
     load_sem, field_send, field_recv, block_send, block_recv, pass_send, pass_recv,
 ):
     fields = (field0, field1, field2, field3)
@@ -43,9 +43,12 @@
         pltpu.make_async_copy(eval_hbm, eval_vmem, load_sem.at[1]),
         pltpu.make_async_copy(near_hbm, near_vmem, load_sem.at[2]),
         pltpu.make_async_copy(translation_hbm, translation_vmem, load_sem.at[3]),
+        pltpu.make_async_copy(density_hbm, density, load_sem.at[4]),
+        pltpu.make_async_copy(clusters_hbm, clusters, load_sem.at[5]),
+        pltpu.make_async_copy(sources_hbm, sources, load_sem.at[6]),
     ]
-    for load in loads:
-        load.start()
+    for number in (4, 0, 5, 6, 1, 2, 3):
+        loads[number].start()
 
     barrier = pltpu.get_barrier_semaphore()
     pl.semaphore_signal(barrier, inc=1, device_id={"loop": other}, device_id_type=MESH)
@@ -59,14 +62,15 @@
     lax.fori_loop(1, wides, greet, 0)
 
     mine = loop * count
+    loads[4].wait()
     for p in range(count):
         field0[mine + p] = jnp.zeros((padded, elements), jnp.bfloat16)
         field0[mine + p, 0:rows, :] = density[:, p * elements : (p + 1) * elements]
-    loads[0].wait()
-    loads[1].wait()
+    for number in (0, 5, 6, 1):
+        loads[number].wait()
     for p in range(count):
         for c in range(CL_DEV):
-            chosen = clusters[0, p] == c
+            chosen = clusters[p] == c
             source_all[c * rank : (c + 1) * rank, p * elements : (p + 1) * elements] = jnp.where(
                 chosen, source_vmem[p], jnp.zeros((rank, elements), jnp.bfloat16)
             )
@@ -184,13 +188,12 @@
     width = CL_DEV * rank
     padded = -(-rows // 16) * 16
     vmem = pl.BlockSpec(memory_space=pltpu.VMEM)
-    smem = pl.BlockSpec(memory_space=pltpu.SMEM)
     anywhere = pl.BlockSpec(memory_space=pl.ANY)
     low, full = jnp.bfloat16, jnp.float32
     return pl.pallas_call(
         functools.partial(kernel, wides, loops, count),
         out_shape=jax.ShapeDtypeStruct((APPLIES, rows, size), low),
-        in_specs=[smem, smem, vmem, anywhere, anywhere, anywhere, anywhere],
+        in_specs=[anywhere] * 7,
         out_specs=vmem,
         scratch_shapes=[pltpu.VMEM((loops * count, padded, elements), low)] * APPLIES
         + [
@@ -199,10 +202,13 @@
             pltpu.VMEM(source_basis.shape, low),
             pltpu.VMEM(translation.shape, low),
             pltpu.VMEM(eval_basis.shape, low),
+            pltpu.VMEM(density.shape, low),
+            pltpu.SMEM(cluster_of.shape, jnp.int32),
+            pltpu.SMEM(near_source.shape, jnp.int32),
             pltpu.VMEM((width, size), low),
             pltpu.VMEM((width, size), low),
             pltpu.VMEM((count, padded, elements), full),
-            pltpu.SemaphoreType.DMA((4,)),
+            pltpu.SemaphoreType.DMA((7,)),
             pltpu.SemaphoreType.DMA((APPLIES,)),
             pltpu.SemaphoreType.DMA((APPLIES,)),
             pltpu.SemaphoreType.DMA((APPLIES,)),
@@ -211,11 +217,11 @@
             pltpu.SemaphoreType.DMA((APPLIES,)),
         ],
         compiler_params=pltpu.CompilerParams(
-            collective_id=0, has_side_effects=True, vmem_limit_bytes=40 * 2**20
+            collective_id=0, has_side_effects=True, vmem_limit_bytes=60 * 2**20
         ),
         name="apply_operator",
     )(
-        cluster_of.reshape(1, count), near_source, density, near_blocks, source_basis,
+        cluster_of, near_source, density, near_blocks, source_basis,
         translation, eval_basis,
     )
 

time: 39.5 us -> 32.6 us (0.83)
  local copies, waits for them, and re-layouts: 8.21 us -> 1.93 us
  Pallas kernels: 31 us -> 30.5 us
    unnamed x14 -> x0, local copies, waits for them, and re-layouts: 7.26 us -> none
    pallas_call x1, local copies, waits for them, and re-layouts: 0.96 us -> 1.93 us  [per_device(): pl.pallas_call(functools.partial(kernel, wides, loops, count), out_shape=...]
    pallas_call x1, Pallas kernels: 31 us -> 30.5 us  [per_device(): pl.pallas_call(functools.partial(kernel, wides, loops, count), out_shape=...]
where the time goes in v2:
time: 32.6 us; the launch traced here: 32.4 us
  Pallas kernels  30.5 us (94%)
  local copies, waits for them, and re-layouts  1.93 us (6%)
    pallas_call x1, Pallas kernels, per_device(): pl.pallas_call(functools.partial(kernel, wides, loops, count), out_shape=...  30.5 us
    pallas_call x1, local copies, waits for them, and re-layouts, per_device(): pl.pallas_call(functools.partial(kernel, wides, loops, count), out_shape=...  1.93 us

profile of v2, /device:TPU:0, one launch (start us, length us, event | category | flops | bytes accessed | tf_op | source)
XLA Modules:
  0.0 32.4 jit_solution(3359352704447578045)
XLA Ops:
  0.0 30.5 %apply_operator.1 = bf16[4,37,1024]{2,1,0:T(8,128)(2,1)} custom-call(s32[4]{0:T(128)} %clusters_hbm.1, s32[4,8]{1,0:T(4,128)} %sources_hbm.1, bf16[37,1024]{1,0:T(8,128)(2,1)} %density_hbm.1, bf16[4,8,256,256]{3,2,1,0:T(8,128)(2,1)} %near_hbm.1, bf16[4,64,256]{2,1,0:T(8,128)(2,1)} %source_hbm.1, bf16[128,2048]{1,0:T(8,128)(2,1)} %translation_hbm.1, ...), custom_call_target="tpu_custom_call" | custom-call | tf_op jit(solution)/shard_map/apply_operator/pallas_call | solution.py:193
  30.5 1.9 %copy.8 = bf16[4,37,1024]{2,0,1:T(4,128)(2,1)} copy(bf16[4,37,1024]{2,1,0:T(8,128)(2,1)} %apply_operator.1) | data formatting | bytes 606208 | tf_op jit(solution)/shard_map/apply_operator/pallas_call | solution.py:193

commit v3 on v2

v3 whole, which is shorter than its diff:
```python
import functools

import jax
import jax.numpy as jnp
from jax import lax
from jax.experimental import pallas as pl
from jax.experimental.pallas import tpu as pltpu
from jax.sharding import PartitionSpec as P

CL_DEV = 2
APPLIES = 4
MESH = pl.DeviceIdType.MESH
NT = (((1,), (1,)), ((), ()))


def dot_nt(a, b):
    return lax.dot_general(a, b, NT, preferred_element_type=jnp.float32)


def kernel(
    wides, loops, count,
    clusters_hbm, sources_hbm, density_hbm, near_hbm, source_hbm, translation_hbm, eval_hbm,
    out,
    field0, field1, field2, field3, gathered, near_vmem, source_vmem, both,
    eval_vmem, density, clusters, sources, source_all, eval_all, near_sum,
    load_sem, field_send, field_recv, block_send, block_recv,
):
    fields = (field0, field1, field2, field3)
    wide = lax.axis_index("wide")
    loop = lax.axis_index("loop")
    other = 1 - loop
    rows = density.shape[0]
    padded, elements = field0.shape[1:]
    near_count = sources.shape[1]
    rank = source_hbm.shape[1]
    width = CL_DEV * rank
    pair = loops * width
    half = max(wides // 2, 1)
    paired = wides & (wides - 1) == 0

    def partner(step):
        flipped, bit = 0, 1
        while bit < wides:
            mine_bit, step_bit = wide // bit % 2, step // bit % 2
            flipped = flipped + bit * (mine_bit + step_bit - 2 * mine_bit * step_bit)
            bit *= 2
        return flipped

    def target(step):
        return partner(step) if paired else lax.rem(wide + step, wides)

    def origin(step):
        return partner(step) if paired else lax.rem(wide - step + wides, wides)

    def each(first, last, body):
        if last - first <= 8:
            for step in reversed(range(first, last)):
                body(step)
        else:
            lax.fori_loop(0, last - first, lambda i, carry: (body(last - 1 - i), carry)[1], 0)

    barrier = pltpu.get_barrier_semaphore()

    def greet(step):
        for l in (loop, other):
            pl.semaphore_signal(
                barrier, inc=1, device_id={"wide": target(step), "loop": l}, device_id_type=MESH
            )

    each(1, wides, greet)
    pl.semaphore_signal(barrier, inc=1, device_id={"loop": other}, device_id_type=MESH)

    loads = [
        pltpu.make_async_copy(source_hbm, source_vmem, load_sem.at[0]),
        pltpu.make_async_copy(eval_hbm, eval_vmem, load_sem.at[1]),
        pltpu.make_async_copy(near_hbm, near_vmem, load_sem.at[2]),
        pltpu.make_async_copy(translation_hbm, both.at[pl.ds(0, width)], load_sem.at[3]),
        pltpu.make_async_copy(density_hbm, density, load_sem.at[4]),
        pltpu.make_async_copy(clusters_hbm, clusters, load_sem.at[5]),
        pltpu.make_async_copy(sources_hbm, sources, load_sem.at[6]),
    ]
    for number in (4, 0, 5, 6, 1, 3, 2):
        loads[number].start()

    mine = loop * count
    loads[4].wait()
    for p in range(count):
        field0[mine + p] = jnp.zeros((padded, elements), jnp.bfloat16)
        field0[mine + p, 0:rows, :] = density[:, p * elements : (p + 1) * elements]
    for number in (0, 5, 6, 1):
        loads[number].wait()
    for p in range(count):
        for c in range(CL_DEV):
            chosen = clusters[p] == c
            source_all[c * rank : (c + 1) * rank, p * elements : (p + 1) * elements] = jnp.where(
                chosen, source_vmem[p], jnp.zeros((rank, elements), jnp.bfloat16)
            )
            eval_all[c * rank : (c + 1) * rank, p * elements : (p + 1) * elements] = jnp.where(
                chosen, eval_vmem[p], jnp.zeros((rank, elements), jnp.bfloat16)
            )
    own = jnp.concatenate([field0[mine + p] for p in range(count)], axis=1)
    gathered[0, loop] = dot_nt(own, source_all[...]).astype(jnp.bfloat16)

    def remote(ref, send, recv, device):
        return pltpu.make_async_remote_copy(
            src_ref=ref[0], dst_ref=ref[1], send_sem=send, recv_sem=recv,
            device_id=device, device_id_type=MESH,
        )

    def field_copy(j):
        part = fields[j].at[pl.ds(mine, count)]
        return remote((part, part), field_send.at[j], field_recv.at[j], {"loop": other})

    def send_blocks(j, first, last):
        def body(step):
            for l in (loop, other):
                remote(
                    (gathered.at[j, loop], gathered.at[j, loops * step + loop]),
                    block_send.at[j], block_recv.at[j, 0 if step_near(step) else 1],
                    {"wide": target(step), "loop": l},
                ).start()

        def step_near(step):
            return last <= half

        each(max(first, 1), last, body)
        if first == 0:
            block = gathered.at[j, loop]
            remote((block, block), block_send.at[j], block_recv.at[j, 0], {"loop": other}).start()

    def wait_blocks(j, first, last, sem):
        ref = gathered.at[j, pl.ds(first, last - first)]
        remote((ref, ref), block_send.at[j], block_recv.at[j, sem], {"loop": other}).wait_recv()

    def translate(j, first, last, high):
        def term(step):
            blocks = [gathered[j, loops * step + l] for l in range(loops)]
            columns = pl.ds(pl.multiple_of(origin(step) * pair, pair), pair)
            return dot_nt(jnp.concatenate(blocks, axis=1), both[0:high, columns])

        if last - first <= 8:
            return sum((term(step) for step in range(first + 1, last)), term(first))
        start = jnp.zeros((padded, high), jnp.float32)
        return lax.fori_loop(first, last, lambda step, total: total + term(step), start)

    pl.semaphore_wait(barrier, loops * wides - 1)
    field_copy(0).start()
    send_blocks(0, half, wides)
    send_blocks(0, 0, half)

    loads[3].wait()
    inner = dot_nt(source_all[...], eval_all[...])
    inner_high = inner.astype(jnp.bfloat16)
    inner_low = (inner - inner_high.astype(jnp.float32)).astype(jnp.bfloat16)
    length = both.shape[1]
    tile = min(length, 2048)
    for start in range(0, length, tile):
        some = both[0:width, start : start + tile]
        both[width:, start : start + tile] = (
            jnp.dot(inner_high, some, preferred_element_type=jnp.float32)
            + jnp.dot(inner_low, some, preferred_element_type=jnp.float32)
        ).astype(jnp.bfloat16)
    loads[2].wait()

    for j in range(APPLIES):
        final = j + 1 == APPLIES
        field = fields[j]
        field_copy(j).wait_recv()
        for p in range(count):
            total = None
            for n in range(near_count):
                term = dot_nt(field[sources[p, n]], near_vmem[p, n])
                total = term if total is None else total + term
            near_sum[p] = total
        if not final:
            own = jnp.concatenate(
                [near_sum[p].astype(jnp.bfloat16) for p in range(count)], axis=1
            )
            near_coeffs = dot_nt(own, source_all[...])

        high = width if final else 2 * width
        wait_blocks(j, 1, loops * half, 0)
        total = translate(j, 0, half, high)
        if wides > half:
            wait_blocks(j, loops * half, loops * wides, 1)
            total = total + translate(j, half, wides, high)
        if not final:
            gathered[j + 1, loop] = (near_coeffs + total[:, width:]).astype(jnp.bfloat16)
            send_blocks(j + 1, half, wides)
        expansion = total[:, :width].astype(jnp.bfloat16)
        for p in range(count):
            far = jnp.dot(
                expansion, eval_all[:, p * elements : (p + 1) * elements],
                preferred_element_type=jnp.float32,
            )
            value = (near_sum[p] + far).astype(jnp.bfloat16)
            if not final:
                fields[j + 1][mine + p] = value
            out[j, :, p * elements : (p + 1) * elements] = value[:rows]
        if not final:
            field_copy(j + 1).start()
            send_blocks(j + 1, 0, half)

    for j in range(APPLIES):
        field_copy(j).wait_send()
        most = gathered.at[j, pl.ds(0, loops * wides - 1)]
        remote((most, most), block_send.at[j], block_recv.at[j, 0], {"loop": other}).wait_send()


def per_device(
    density, near_blocks, near_source, source_basis, cluster_of, translation, eval_basis
):
    wides, loops = lax.axis_size("wide"), lax.axis_size("loop")
    rows, size = density.shape
    count, near_count, elements, _ = near_blocks.shape
    rank = source_basis.shape[1]
    width = CL_DEV * rank
    padded = -(-rows // 16) * 16
    vmem = pl.BlockSpec(memory_space=pltpu.VMEM)
    anywhere = pl.BlockSpec(memory_space=pl.ANY)
    low, full = jnp.bfloat16, jnp.float32
    return pl.pallas_call(
        functools.partial(kernel, wides, loops, count),
        out_shape=jax.ShapeDtypeStruct((APPLIES, rows, size), low),
        in_specs=[anywhere] * 7,
        out_specs=vmem,
        scratch_shapes=[pltpu.VMEM((loops * count, padded, elements), low)] * APPLIES
        + [
            pltpu.VMEM((APPLIES, loops * wides, padded, width), low),
            pltpu.VMEM(near_blocks.shape, low),
            pltpu.VMEM(source_basis.shape, low),
            pltpu.VMEM((2 * width, translation.shape[1]), low),
            pltpu.VMEM(eval_basis.shape, low),
            pltpu.VMEM(density.shape, low),
            pltpu.SMEM(cluster_of.shape, jnp.int32),
            pltpu.SMEM(near_source.shape, jnp.int32),
            pltpu.VMEM((width, size), low),
            pltpu.VMEM((width, size), low),
            pltpu.VMEM((count, padded, elements), full),
            pltpu.SemaphoreType.DMA((7,)),
            pltpu.SemaphoreType.DMA((APPLIES,)),
            pltpu.SemaphoreType.DMA((APPLIES,)),
            pltpu.SemaphoreType.DMA((APPLIES,)),
            pltpu.SemaphoreType.DMA((APPLIES, 2)),
        ],
        compiler_params=pltpu.CompilerParams(
            collective_id=0, has_side_effects=True, vmem_limit_bytes=60 * 2**20
        ),
        name="apply_operator",
    )(
        cluster_of, near_source, density, near_blocks, source_basis,
        translation, eval_basis,
    )


def solution(mesh):
    split = ("parts", "wide", "loop")
    return jax.shard_map(
        per_device,
        mesh=mesh,
        in_specs=(
            P(None, split),
            P(split, None, None, None),
            P(split, None),
            P(split, None, None),
            P(split),
            P(split, None),
            P(split, None, None),
        ),
        out_specs=P(None, None, split),
        check_vma=False,
    )
```

time: 32.6 us -> 35.2 us (1.080)
  Pallas kernels: 30.5 us -> 33.1 us
    pallas_call x1, Pallas kernels: 30.5 us -> 33.1 us  [per_device(): pl.pallas_call(functools.partial(kernel, wides, loops, count), out_shape=...]
where the time goes in v3:
time: 35.2 us; the launch traced here: 35 us
  Pallas kernels  33.1 us (94%)
  local copies, waits for them, and re-layouts  1.93 us (5%)
    pallas_call x1, Pallas kernels, per_device(): pl.pallas_call(functools.partial(kernel, wides, loops, count), out_shape=...  33.1 us
    pallas_call x1, local copies, waits for them, and re-layouts, per_device(): pl.pallas_call(functools.partial(kernel, wides, loops, count), out_shape=...  1.93 us

profile of v3, /device:TPU:0, one launch (start us, length us, event | category | flops | bytes accessed | tf_op | source)
XLA Modules:
  0.0 35.0 jit_solution(13078782266601437327)
XLA Ops:
  0.0 33.1 %apply_operator.1 = bf16[4,37,1024]{2,1,0:T(8,128)(2,1)} custom-call(s32[4]{0:T(128)} %clusters_hbm.1, s32[4,8]{1,0:T(4,128)} %sources_hbm.1, bf16[37,1024]{1,0:T(8,128)(2,1)} %density_hbm.1, bf16[4,8,256,256]{3,2,1,0:T(8,128)(2,1)} %near_hbm.1, bf16[4,64,256]{2,1,0:T(8,128)(2,1)} %source_hbm.1, bf16[128,2048]{1,0:T(8,128)(2,1)} %translation_hbm.1, ...), custom_call_target="tpu_custom_call" | custom-call | tf_op jit(solution)/shard_map/apply_operator/pallas_call | solution.py:222
  33.1 1.9 %copy.8 = bf16[4,37,1024]{2,0,1:T(4,128)(2,1)} copy(bf16[4,37,1024]{2,1,0:T(8,128)(2,1)} %apply_operator.1) | data formatting | bytes 606208 | tf_op jit(solution)/shard_map/apply_operator/pallas_call | solution.py:222

commit v4 on v3

--- a/solution.py
+++ b/solution.py
@@ -23,7 +23,7 @@
     out,
     field0, field1, field2, field3, gathered, near_vmem, source_vmem, both,
     eval_vmem, density, clusters, sources, source_all, eval_all, near_sum,
-    load_sem, field_send, field_recv, block_send, block_recv,
+    load_sem, field_send, field_recv, block_send, near_recv, far_recv, pass_send, pass_recv,
 ):
     fields = (field0, field1, field2, field3)
     wide = lax.axis_index("wide")
@@ -35,7 +35,7 @@
     rank = source_hbm.shape[1]
     width = CL_DEV * rank
     pair = loops * width
-    half = max(wides // 2, 1)
+    close = max(wides // 4, 1)
     paired = wides & (wides - 1) == 0
 
     def partner(step):
@@ -62,12 +62,18 @@
     barrier = pltpu.get_barrier_semaphore()
 
     def greet(step):
-        for l in (loop, other):
-            pl.semaphore_signal(
-                barrier, inc=1, device_id={"wide": target(step), "loop": l}, device_id_type=MESH
-            )
-
-    each(1, wides, greet)
+        pl.semaphore_signal(
+            barrier, inc=1, device_id={"wide": target(step)}, device_id_type=MESH
+        )
+
+    def greet_both(step):
+        greet(step)
+        pl.semaphore_signal(
+            barrier, inc=1, device_id={"wide": target(step), "loop": other}, device_id_type=MESH
+        )
+
+    each(close, wides, greet)
+    each(1, close, greet_both)
     pl.semaphore_signal(barrier, inc=1, device_id={"loop": other}, device_id_type=MESH)
 
     loads = [
@@ -99,7 +105,7 @@
                 chosen, eval_vmem[p], jnp.zeros((rank, elements), jnp.bfloat16)
             )
     own = jnp.concatenate([field0[mine + p] for p in range(count)], axis=1)
-    gathered[0, loop] = dot_nt(own, source_all[...]).astype(jnp.bfloat16)
+    gathered[0, loop, 0] = dot_nt(own, source_all[...]).astype(jnp.bfloat16)
 
     def remote(ref, send, recv, device):
         return pltpu.make_async_remote_copy(
@@ -111,42 +117,76 @@
         part = fields[j].at[pl.ds(mine, count)]
         return remote((part, part), field_send.at[j], field_recv.at[j], {"loop": other})
 
-    def send_blocks(j, first, last):
+    def send_far(j):
         def body(step):
-            for l in (loop, other):
-                remote(
-                    (gathered.at[j, loop], gathered.at[j, loops * step + loop]),
-                    block_send.at[j], block_recv.at[j, 0 if step_near(step) else 1],
-                    {"wide": target(step), "loop": l},
-                ).start()
-
-        def step_near(step):
-            return last <= half
-
-        each(max(first, 1), last, body)
-        if first == 0:
-            block = gathered.at[j, loop]
-            remote((block, block), block_send.at[j], block_recv.at[j, 0], {"loop": other}).start()
-
-    def wait_blocks(j, first, last, sem):
-        ref = gathered.at[j, pl.ds(first, last - first)]
-        remote((ref, ref), block_send.at[j], block_recv.at[j, sem], {"loop": other}).wait_recv()
-
-    def translate(j, first, last, high):
-        def term(step):
-            blocks = [gathered[j, loops * step + l] for l in range(loops)]
-            columns = pl.ds(pl.multiple_of(origin(step) * pair, pair), pair)
-            return dot_nt(jnp.concatenate(blocks, axis=1), both[0:high, columns])
-
+            remote(
+                (gathered.at[j, loop, 0], gathered.at[j, loop, step]),
+                block_send.at[j], far_recv.at[j, step], {"wide": target(step)},
+            ).start()
+
+        each(close, wides, body)
+
+    def send_near(j):
+        def body(step):
+            ref = (gathered.at[j, loop, 0], gathered.at[j, loop, step])
+            remote(
+                ref, block_send.at[j], near_recv.at[j, 0], {"wide": target(step)}
+            ).start()
+            remote(
+                ref, block_send.at[j], near_recv.at[j, 1], {"wide": target(step), "loop": other}
+            ).start()
+
+        each(1, close, body)
+        block = gathered.at[j, loop, 0]
+        remote((block, block), block_send.at[j], near_recv.at[j, 1], {"loop": other}).start()
+
+    def arrive(ref, sem):
+        remote((ref, ref), block_send.at[0], sem, {"loop": other}).wait_recv()
+
+    def pass_far(j):
+        def body(step):
+            block = gathered.at[j, loop, step]
+            arrive(block, far_recv.at[j, step])
+            remote((block, block), pass_send.at[j], pass_recv.at[j], {"loop": other}).start()
+
+        lax.fori_loop(close, wides, lambda step, carry: (body(step), carry)[1], 0, unroll=wides <= 8)
+
+    def columns(step, l):
+        return pl.ds(pl.multiple_of(origin(step) * pair + l * width, width), width)
+
+    def summed(first, last, term, high):
         if last - first <= 8:
             return sum((term(step) for step in range(first + 1, last)), term(first))
         start = jnp.zeros((padded, high), jnp.float32)
         return lax.fori_loop(first, last, lambda step, total: total + term(step), start)
 
-    pl.semaphore_wait(barrier, loops * wides - 1)
+    def translate_near(j, high):
+        def term(step):
+            blocks = [gathered[j, l, step] for l in range(loops)]
+            some = pl.ds(pl.multiple_of(origin(step) * pair, pair), pair)
+            return dot_nt(jnp.concatenate(blocks, axis=1), both[0:high, some])
+
+        return summed(0, close, term, high)
+
+    def translate_far(j, l, high):
+        if close % 2:
+            def single(step):
+                return dot_nt(gathered[j, l, step], both[0:high, columns(step, l)])
+
+            return summed(close, wides, single, high)
+
+        def term(at):
+            steps = (2 * at, 2 * at + 1)
+            blocks = [gathered[j, l, step] for step in steps]
+            parts = [both[0:high, columns(step, l)] for step in steps]
+            return dot_nt(jnp.concatenate(blocks, axis=1), jnp.concatenate(parts, axis=1))
+
+        return summed(close // 2, wides // 2, term, high)
+
+    pl.semaphore_wait(barrier, wides - 1 + close)
     field_copy(0).start()
-    send_blocks(0, half, wides)
-    send_blocks(0, 0, half)
+    send_far(0)
+    send_near(0)
 
     loads[3].wait()
     inner = dot_nt(source_all[...], eval_all[...])
@@ -179,14 +219,18 @@
             near_coeffs = dot_nt(own, source_all[...])
 
         high = width if final else 2 * width
-        wait_blocks(j, 1, loops * half, 0)
-        total = translate(j, 0, half, high)
-        if wides > half:
-            wait_blocks(j, loops * half, loops * wides, 1)
-            total = total + translate(j, half, wides, high)
+        if close > 1:
+            arrive(gathered.at[j, loop, pl.ds(1, close - 1)], near_recv.at[j, 0])
+        arrive(gathered.at[j, other, pl.ds(0, close)], near_recv.at[j, 1])
+        total = translate_near(j, high)
+        if wides > close:
+            pass_far(j)
+            total = total + translate_far(j, loop, high)
+            arrive(gathered.at[j, other, pl.ds(close, wides - close)], pass_recv.at[j])
+            total = total + translate_far(j, other, high)
         if not final:
-            gathered[j + 1, loop] = (near_coeffs + total[:, width:]).astype(jnp.bfloat16)
-            send_blocks(j + 1, half, wides)
+            gathered[j + 1, loop, 0] = (near_coeffs + total[:, width:]).astype(jnp.bfloat16)
+            send_far(j + 1)
         expansion = total[:, :width].astype(jnp.bfloat16)
         for p in range(count):
             far = jnp.dot(
@@ -199,12 +243,17 @@
             out[j, :, p * elements : (p + 1) * elements] = value[:rows]
         if not final:
             field_copy(j + 1).start()
-            send_blocks(j + 1, 0, half)
+            send_near(j + 1)
 
     for j in range(APPLIES):
         field_copy(j).wait_send()
-        most = gathered.at[j, pl.ds(0, loops * wides - 1)]
-        remote((most, most), block_send.at[j], block_recv.at[j, 0], {"loop": other}).wait_send()
+        sent = [
+            (gathered.at[j, 0], block_send), (gathered.at[j, 0, pl.ds(0, close - 1)], block_send),
+            (gathered.at[j, 0, pl.ds(0, wides - close)], pass_send),
+        ]
+        for ref, sem in sent:
+            if ref.shape[0]:
+                remote((ref, ref), sem.at[j], near_recv.at[j, 0], {"loop": other}).wait_send()
 
 
 def per_device(
@@ -226,7 +275,7 @@
         out_specs=vmem,
         scratch_shapes=[pltpu.VMEM((loops * count, padded, elements), low)] * APPLIES
         + [
-            pltpu.VMEM((APPLIES, loops * wides, padded, width), low),
+            pltpu.VMEM((APPLIES, loops, wides, padded, width), low),
             pltpu.VMEM(near_blocks.shape, low),
             pltpu.VMEM(source_basis.shape, low),
             pltpu.VMEM((2 * width, translation.shape[1]), low),
@@ -242,6 +291,9 @@
             pltpu.SemaphoreType.DMA((APPLIES,)),
             pltpu.SemaphoreType.DMA((APPLIES,)),
             pltpu.SemaphoreType.DMA((APPLIES, 2)),
+            pltpu.SemaphoreType.DMA((APPLIES, wides)),
+            pltpu.SemaphoreType.DMA((APPLIES,)),
+            pltpu.SemaphoreType.DMA((APPLIES,)),
         ],
         compiler_params=pltpu.CompilerParams(
             collective_id=0, has_side_effects=True, vmem_limit_bytes=60 * 2**20

time: 35.2 us -> 31 us (0.88)
  Pallas kernels: 33.1 us -> 28.9 us
    pallas_call x1, Pallas kernels: 33.1 us -> 28.9 us  [per_device(): pl.pallas_call(functools.partial(kernel, wides, loops, count), out_shape=...]
where the time goes in v4:
time: 31 us; the launch traced here: 30.8 us
  Pallas kernels  28.9 us (93%)
  local copies, waits for them, and re-layouts  1.93 us (6%)
    pallas_call x1, Pallas kernels, per_device(): pl.pallas_call(functools.partial(kernel, wides, loops, count), out_shape=...  28.9 us
    pallas_call x1, local copies, waits for them, and re-layouts, per_device(): pl.pallas_call(functools.partial(kernel, wides, loops, count), out_shape=...  1.93 us

profile of v4, /device:TPU:0, one launch (start us, length us, event | category | flops | bytes accessed | tf_op | source)
XLA Modules:
  0.0 30.8 jit_solution(11958824005316760401)
XLA Ops:
  0.0 28.9 %apply_operator.1 = bf16[4,37,1024]{2,1,0:T(8,128)(2,1)} custom-call(s32[4]{0:T(128)} %clusters_hbm.1, s32[4,8]{1,0:T(4,128)} %sources_hbm.1, bf16[37,1024]{1,0:T(8,128)(2,1)} %density_hbm.1, bf16[4,8,256,256]{3,2,1,0:T(8,128)(2,1)} %near_hbm.1, bf16[4,64,256]{2,1,0:T(8,128)(2,1)} %source_hbm.1, bf16[128,2048]{1,0:T(8,128)(2,1)} %translation_hbm.1, ...), custom_call_target="tpu_custom_call" | custom-call | tf_op jit(solution)/shard_map/apply_operator/pallas_call | solution.py:271
  28.9 1.9 %copy.8 = bf16[4,37,1024]{2,0,1:T(4,128)(2,1)} copy(bf16[4,37,1024]{2,1,0:T(8,128)(2,1)} %apply_operator.1) | data formatting | bytes 606208 | tf_op jit(solution)/shard_map/apply_operator/pallas_call | solution.py:271

commit v5 on v4

--- a/solution.py
+++ b/solution.py
@@ -20,10 +20,10 @@
 def kernel(
     wides, loops, count,
     clusters_hbm, sources_hbm, density_hbm, near_hbm, source_hbm, translation_hbm, eval_hbm,
-    out,
+    out_hbm,
     field0, field1, field2, field3, gathered, near_vmem, source_vmem, both,
-    eval_vmem, density, clusters, sources, source_all, eval_all, near_sum,
-    load_sem, field_send, field_recv, block_send, near_recv, far_recv, pass_send, pass_recv,
+    eval_vmem, density, clusters, sources, source_all, eval_all, near_sum, out,
+    load_sem, store_sem, field_send, field_recv, block_send, near_recv, far_recv, pass_send, pass_recv,
 ):
     fields = (field0, field1, field2, field3)
     wide = lax.axis_index("wide")
@@ -144,12 +144,11 @@
         remote((ref, ref), block_send.at[0], sem, {"loop": other}).wait_recv()
 
     def pass_far(j):
-        def body(step):
-            block = gathered.at[j, loop, step]
-            arrive(block, far_recv.at[j, step])
+        cut = (close + wides) // 2
+        for low, high in ((close, cut), (cut, wides)):
+            each(low, high, lambda step: arrive(gathered.at[j, loop, step], far_recv.at[j, step]))
+            block = gathered.at[j, loop, pl.ds(low, high - low)]
             remote((block, block), pass_send.at[j], pass_recv.at[j], {"loop": other}).start()
-
-        lax.fori_loop(close, wides, lambda step, carry: (body(step), carry)[1], 0, unroll=wides <= 8)
 
     def columns(step, l):
         return pl.ds(pl.multiple_of(origin(step) * pair + l * width, width), width)
@@ -184,8 +183,8 @@
         return summed(close // 2, wides // 2, term, high)
 
     pl.semaphore_wait(barrier, wides - 1 + close)
+    send_far(0)
     field_copy(0).start()
-    send_far(0)
     send_near(0)
 
     loads[3].wait()
@@ -202,6 +201,9 @@
         ).astype(jnp.bfloat16)
     loads[2].wait()
 
+    stores = [
+        pltpu.make_async_copy(out.at[j], out_hbm.at[j], store_sem.at[j]) for j in range(APPLIES)
+    ]
     for j in range(APPLIES):
         final = j + 1 == APPLIES
         field = fields[j]
@@ -241,11 +243,13 @@
             if not final:
                 fields[j + 1][mine + p] = value
             out[j, :, p * elements : (p + 1) * elements] = value[:rows]
+        stores[j].start()
         if not final:
             field_copy(j + 1).start()
             send_near(j + 1)
 
     for j in range(APPLIES):
+        stores[j].wait()
         field_copy(j).wait_send()
         sent = [
             (gathered.at[j, 0], block_send), (gathered.at[j, 0, pl.ds(0, close - 1)], block_send),
@@ -265,14 +269,13 @@
     rank = source_basis.shape[1]
     width = CL_DEV * rank
     padded = -(-rows // 16) * 16
-    vmem = pl.BlockSpec(memory_space=pltpu.VMEM)
     anywhere = pl.BlockSpec(memory_space=pl.ANY)
     low, full = jnp.bfloat16, jnp.float32
     return pl.pallas_call(
         functools.partial(kernel, wides, loops, count),
         out_shape=jax.ShapeDtypeStruct((APPLIES, rows, size), low),
         in_specs=[anywhere] * 7,
-        out_specs=vmem,
+        out_specs=anywhere,
         scratch_shapes=[pltpu.VMEM((loops * count, padded, elements), low)] * APPLIES
         + [
             pltpu.VMEM((APPLIES, loops, wides, padded, width), low),
@@ -286,7 +289,9 @@
             pltpu.VMEM((width, size), low),
             pltpu.VMEM((width, size), low),
             pltpu.VMEM((count, padded, elements), full),
+            pltpu.VMEM((APPLIES, rows, size), low),
             pltpu.SemaphoreType.DMA((7,)),
+            pltpu.SemaphoreType.DMA((APPLIES,)),
             pltpu.SemaphoreType.DMA((APPLIES,)),
             pltpu.SemaphoreType.DMA((APPLIES,)),
             pltpu.SemaphoreType.DMA((APPLIES,)),

time: 31 us -> 30.7 us (level)
  no operation moved by 1% of the time
where the time goes in v5:
time: 30.7 us; the launch traced here: 30.6 us
  Pallas kernels  28.7 us (93%)
  local copies, waits for them, and re-layouts  1.93 us (6%)
    pallas_call x1, Pallas kernels, per_device(): pl.pallas_call(functools.partial(kernel, wides, loops, count), out_shape=...  28.7 us
    pallas_call x1, local copies, waits for them, and re-layouts, per_device(): pl.pallas_call(functools.partial(kernel, wides, loops, count), out_shape=...  1.93 us

profile of v5, /device:TPU:0, one launch (start us, length us, event | category | flops | bytes accessed | tf_op | source)
XLA Modules:
  0.0 30.6 jit_solution(5543332913562367457)
XLA Ops:
  0.0 28.7 %apply_operator.1 = bf16[4,37,1024]{2,1,0:T(8,128)(2,1)} custom-call(s32[4]{0:T(128)} %clusters_hbm.1, s32[4,8]{1,0:T(4,128)} %sources_hbm.1, bf16[37,1024]{1,0:T(8,128)(2,1)} %density_hbm.1, bf16[4,8,256,256]{3,2,1,0:T(8,128)(2,1)} %near_hbm.1, bf16[4,64,256]{2,1,0:T(8,128)(2,1)} %source_hbm.1, bf16[128,2048]{1,0:T(8,128)(2,1)} %translation_hbm.1, ...), custom_call_target="tpu_custom_call" | custom-call | tf_op jit(solution)/shard_map/apply_operator/pallas_call | solution.py:274
  28.7 1.9 %copy.8 = bf16[4,37,1024]{2,0,1:T(4,128)(2,1)} copy(bf16[4,37,1024]{2,1,0:T(8,128)(2,1)} %apply_operator.1) | data formatting | bytes 606208 | tf_op jit(solution)/shard_map/apply_operator/pallas_call | solution.py:274
